TPU v7x, 128 devices: a whole 4x4x4 slice. The times are simulated.
128 devices in a mesh: clip: 4 (over y), seq: 32 (over x, z, core).
Axes of the slice: x: 4, y: 4, z: 4, core: 2. Of those that a mesh axis runs over, the one named last changes fastest.
Arguments:
- tokens: bfloat16 [327680, 1280], P(('clip', 'seq')), parts along dimension 0, may hold values from -6 to 6
- slot_proj: bfloat16 [1280, 64], replicated, may hold values from -5 to 5, as said below
- w_in: bfloat16 [32, 1280, 2560], P('seq'), may hold values from -0.15625 to 0.15625
- w_out: bfloat16 [32, 2560, 1280], P('seq'), may hold values from -0.125 to 0.125
Outputs:
- mixed: bfloat16 [327680, 1280], P(('clip', 'seq')), parts along dimension 0
There are 4 independent parts, one for each index of `clip`. A program takes and returns all parts, laid end to end along the dimension named above; an argument that names none is the same for every part. Nothing has to cross between parts.
Inputs may be any that keep to these rules, and one draw needn't show every extreme that they name: `slot_proj`: the slots' parameters.
All inputs are finite; a program needn't handle non-finite values.
Results may differ from a plain program's by a relative error of at most 0.02.
Values may be sent and summed in bfloat16 or wider, within the bound.
No kernel may reach another device: no remote copies, remote signals or barrier semaphores. Data moves between devices by JAX's collectives and lax.ppermute only.
A program may use at most 64 MiB of HBM per device.

v0:
```python
import jax
import jax.numpy as jnp
from jax import lax
from jax.sharding import PartitionSpec as P

SLOTS = 2


def body(tokens, slot_proj, w_in, w_out):
    logits = jnp.dot(tokens, slot_proj, preferred_element_type=jnp.float32)
    own_rows = w_in.shape[0] * SLOTS
    start_row = lax.axis_index("seq") * own_rows
    width = tokens.shape[1]
    col_max = lax.pmax(jnp.max(logits, axis=0), "seq")
    shifted = jnp.exp(logits - col_max[None, :])
    dispatch = shifted.astype(jnp.bfloat16)
    part_total = jnp.sum(shifted, axis=0)
    col_total = lax.psum(part_total, "seq")
    full_num = lax.dot_general(
        dispatch, tokens, (((0,), (0,)), ((), ())), preferred_element_type=jnp.float32
    )
    num_all = lax.psum(full_num.astype(jnp.bfloat16), "seq").astype(jnp.float32)
    own_total = lax.dynamic_slice_in_dim(col_total, start_row, own_rows, 0)
    own_num = lax.dynamic_slice_in_dim(num_all, start_row, own_rows, 0)
    slot_in = (own_num / own_total[:, None]).astype(jnp.bfloat16)
    slot_in = slot_in.reshape(w_in.shape[0], SLOTS, width)
    hidden = jax.nn.gelu(
        jnp.einsum("esd,edf->esf", slot_in, w_in, preferred_element_type=jnp.float32)
    ).astype(jnp.bfloat16)
    slot_out = jnp.einsum("esf,efd->esd", hidden, w_out, preferred_element_type=jnp.float32).astype(
        jnp.bfloat16
    )
    slot_out = slot_out.reshape(own_rows, width)
    combine = jax.nn.softmax(logits, axis=1).astype(jnp.bfloat16)
    mixed = jnp.dot(
        combine,
        lax.all_gather(slot_out, "seq", axis=0, tiled=True),
        preferred_element_type=jnp.float32,
    )
    return mixed.astype(jnp.bfloat16)


def solution(mesh):
    return jax.shard_map(
        body,
        mesh=mesh,
        in_specs=(P(("clip", "seq"), None), P(), P("seq", None, None), P("seq", None, None)),
        out_specs=P(("clip", "seq"), None),
        check_vma=False,
    )
```

profile of v0, /device:TPU:1, one launch (start us, length us, event | category | flops | bytes accessed | tf_op | source)
XLA Modules:
  0.0 223.0 jit_solution(15240578596407113539)
XLA Ops:
  6.5 0.0 copy-start
  6.5 0.0 all-reduce.2.cloned.1.call-start
  6.5 0.9 copy-done
  7.5 5.0 %fusion.48 = (f32[2560]{0:T(1024)S(1)}, f32[64]{0:T(128)S(1)}, f32[2560,64]{0,1:T(8,128)S(1)}) fusion(bf16[2560,1280]{1,0:T(8,128)(2,1)} %param.4, bf16[1280,64]{0,1:T(8,128)(2,1)S(1)} %copy-done), kind=kOutput, calls=%fused_computation.39 | convolution fusion | flops 419755456 | bytes 7383296 | tf_op jit(solution)/shard_map/dot_general | solution.py:10
  12.5 64.8 %pmax.7 = f32[64]{0:T(128)S(1)} all-reduce(f32[64]{0:T(128)S(1)} %get-tuple-element.8), channel_id=1, replica_groups=mesh['clip'=4,'seq'=32] {'seq'}, use_global_device_ids=true, to_apply=%region_3.0 | all-reduce | flops 64 | bytes 512 | tf_op jit(solution)/shard_map/pmax | solution.py:14
  77.3 4.8 %convolution_convert_fusion.1 = bf16[64,1280]{1,0:T(8,128)(2,1)} fusion(bf16[2560,1280]{1,0:T(8,128)(2,1)} %param.4, f32[2560,64]{0,1:T(8,128)S(1)} %get-tuple-element.9, f32[64]{0:T(128)S(1)} %pmax.7), kind=kOutput, calls=%fused_computation.5 | convolution fusion | flops 419840000 | bytes 7373056 | tf_op jit(solution)/shard_map/dot_general | solution.py:19
  82.1 0.0 all-reduce.2.cloned.1.call-update
  82.2 0.3 fusion.10
  82.5 67.0 %psum.15 = f32[64]{0:T(128)S(1)} all-reduce(f32[64]{0:T(128)S(1)} %get-tuple-element.6), channel_id=1, replica_groups=mesh['clip'=4,'seq'=32] {'seq'}, use_global_device_ids=true, to_apply=%region_6.0 | all-reduce | flops 64 | bytes 512 | tf_op jit(solution)/shard_map/psum | solution.py:18
  149.5 0.1 dynamic_slice.7
  149.6 32.2 %all-reduce.2.cloned.1.call-done = bf16[64,1280]{1,0:T(8,128)(2,1)} async-done(((bf16[64,1280]{1,0:T(8,128)(2,1)}), bf16[64,1280]{1,0:T(8,128)(2,1)}) %all-reduce.2.cloned.1.call-update) | async-done | bytes 163856 | tf_op jit(solution)/shard_map/psum | solution.py:22
  181.8 6.7 %fusion.7 = bf16[1,2,1280]{2,1,0:T(2,128)(2,1)S(1)} fusion(bf16[1,2560,1280]{2,1,0:T(8,128)(2,1)} %param.7, bf16[1,1280,2560]{2,1,0:T(8,128)(2,1)} %param.6, f32[2]{0:T(128)S(1)} %dynamic_slice.7, bf16[64,1280]{1,0:T(8,128)(2,1)} %all-reduce.2.cloned.1.call-done, s32[]{:T(128)S(6)} %select_n.4), kind=kOutput, calls=%fused_computation.7 | convolution fusion | flops 26270720 | bytes 13117452 | tf_op jit(solution)/shard_map/esf,efd->esd/dot_general | solution.py:30
  188.5 22.8 %all-gather = bf16[32,2,1280]{2,1,0:T(2,128)(2,1)S(1)} all-gather(bf16[1,2,1280]{2,1,0:T(2,128)(2,1)S(1)} %fusion.7), channel_id=1, replica_groups=mesh['clip'=4,'seq'=32] {'seq'}, dimensions={0}, use_global_device_ids=true | all-gather | bytes 168960 | tf_op jit(solution)/shard_map/all_gather | solution.py:37
  211.3 0.1 reshape.33
  211.4 4.7 %convolution_convert_fusion = bf16[2560,1280]{1,0:T(8,128)(2,1)} fusion(bf16[64,1280]{1,0:T(8,128)(2,1)S(1)} %reshape.33, f32[2560,64]{0,1:T(8,128)S(1)} %get-tuple-element.9, f32[2560]{0:T(1024)S(1)} %get-tuple-element.5, f32[2560]{0:T(1024)S(1)} %get-tuple-element.7), kind=kOutput, calls=%fused_computation | convolution fusion | flops 423198720 | bytes 7393280 | tf_op jit(solution)/shard_map/dot_general | solution.py:35
Async XLA Ops:
  6.5 0.9 copy-start
  6.5 175.2 %all-reduce.2.cloned.1.call-start = ((), (), s32[]{:S(2)}) async-start(), calls=%async_computation | async-start | bytes 327680 | tf_op jit(solution)/shard_map/psum | solution.py:22
Sparse Core Ops, SparseCore 0:
  82.3 99.4 all-reduce.1
where the time goes:
time: 223 us
  blocking collectives  155 us (70%)
  waiting for transfers between devices  32.2 us (14%)
  matrix products  21.3 us (10%)
  between operations  13.4 us (6%)
    psum x1, blocking collectives, body(): col_total = lax.psum(part_total, 'seq')  67 us
    pmax x1, blocking collectives, body(): col_max = lax.pmax(jnp.max(logits, axis=0), 'seq')  64.8 us
    psum x1, waiting for transfers between devices, body(): num_all = lax.psum(full_num.astype(jnp.bfloat16), 'seq').astype(jnp.float32)  32.2 us
    all_gather x1, blocking collectives, body(): lax.all_gather(slot_out, 'seq', axis=0, tiled=True)  22.8 us
    dot_general x1, matrix products, body(): jnp.einsum('esf,efd->esd', hidden, w_out, preferred_element_type=jnp.floa...  6.71 us
    dot_general x1, matrix products, body(): logits = jnp.dot(tokens, slot_proj, preferred_element_type=jnp.float32)  5.04 us
    dot_general x1, matrix products, body(): lax.dot_general(dispatch, tokens, (((0,), (0,)), ((), ())), preferred_ele...  4.83 us
    dot_general x1, matrix products, body(): jnp.dot(combine, lax.all_gather(slot_out, 'seq', axis=0, tiled=True), pre...  4.71 us
  transfers between devices with their start and end apart: 1, of which 1 were waited for; matrix products, arithmetic and copies ran while one was open for 0% of the time, Pallas kernels for 0%

commit v1 on v0

v1 whole, which is shorter than its diff:
```python
import jax
import jax.numpy as jnp
from jax import lax
from jax.sharding import PartitionSpec as P

SLOTS = 2
LANES = 128


def split3(x):
    hi = lax.reduce_precision(x, 8, 7)
    mid = lax.reduce_precision(x - hi, 8, 7)
    return [hi, mid, x - hi - mid]


def body(tokens, slot_proj, w_in, w_out):
    devices = lax.axis_size("seq")
    width = tokens.shape[1]
    logits = jnp.dot(tokens, slot_proj, preferred_element_type=jnp.float32)
    own_max = jnp.max(logits, axis=0)
    shifted = jnp.exp(logits - own_max[None, :])
    own_total = jnp.sum(shifted, axis=0)
    own_num = lax.dot_general(
        shifted.astype(jnp.bfloat16), tokens, (((0,), (0,)), ((), ())), preferred_element_type=jnp.float32
    )
    stats = jnp.stack(split3(own_max) + split3(own_total), axis=1)
    stats = jnp.pad(stats, ((0, 0), (0, LANES - stats.shape[1])))
    sent = jnp.concatenate([own_num, stats], axis=1).astype(jnp.bfloat16)
    got = lax.all_to_all(sent.reshape(devices, -1, width + LANES), "seq", 0, 0).astype(jnp.float32)
    maxes = got[:, :, width] + got[:, :, width + 1] + got[:, :, width + 2]
    totals = got[:, :, width + 3] + got[:, :, width + 4] + got[:, :, width + 5]
    scale = jnp.exp(maxes - jnp.max(maxes, axis=0)[None])
    num = jnp.sum(got[:, :, :width] * scale[:, :, None], axis=0)
    slot_in = (num / jnp.sum(totals * scale, axis=0)[:, None]).astype(jnp.bfloat16)
    slot_in = slot_in.reshape(w_in.shape[0], SLOTS, width)
    hidden = jax.nn.gelu(
        jnp.einsum("esd,edf->esf", slot_in, w_in, preferred_element_type=jnp.float32)
    ).astype(jnp.bfloat16)
    slot_out = jnp.einsum("esf,efd->esd", hidden, w_out, preferred_element_type=jnp.float32).astype(
        jnp.bfloat16
    )
    slot_out = slot_out.reshape(1, -1, width)
    slot_all = lax.all_to_all(jnp.broadcast_to(slot_out, (devices, *slot_out.shape[1:])), "seq", 0, 0)
    combine = jax.nn.softmax(logits, axis=1).astype(jnp.bfloat16)
    mixed = jnp.dot(combine, slot_all.reshape(-1, width), preferred_element_type=jnp.float32)
    return mixed.astype(jnp.bfloat16)


def solution(mesh):
    return jax.shard_map(
        body,
        mesh=mesh,
        in_specs=(P(("clip", "seq"), None), P(), P("seq", None, None), P("seq", None, None)),
        out_specs=P(("clip", "seq"), None),
        check_vma=False,
    )
```

time: 223 us -> 53.5 us (0.24)
  blocking collectives: 155 us -> 28.9 us
  waiting for transfers between devices: 32.2 us -> 0 us
  between operations: 13.4 us -> 0.09 us
  other arithmetic: 0.3 us -> 3.64 us
  matrix products: 21.3 us -> 18.3 us
    psum x1 -> x0, blocking collectives: 67 us -> none  [body(): col_total = lax.psum(part_total, 'seq')]
    pmax x1 -> x0, blocking collectives: 64.8 us -> none  [body(): col_max = lax.pmax(jnp.max(logits, axis=0), 'seq')]
    psum x1 -> x0, waiting for transfers between devices: 32.2 us -> none  [body(): num_all = lax.psum(full_num.astype(jnp.bfloat16), 'seq').astype(jnp.float32)]
    all_to_all x0 -> x2, blocking collectives: none -> 28.9 us  [the longest x1 17.4 us: body(): lax.all_to_all(sent.reshape(devices, -1, width + LANES), 'seq', 0, 0)]
    all_gather x1 -> x0, blocking collectives: 22.8 us -> none  [body(): lax.all_gather(slot_out, 'seq', axis=0, tiled=True)]
    dot_general x2, matrix products: 9.54 us -> 6.03 us  [the longest x1 4.71 us: body(): jnp.dot(combine, slot_all.reshape(-1, width), preferred_element_type=jnp....]
    reduce_sum x0 -> x2, other arithmetic: none -> 2.43 us  [the longest x1 2.24 us: body(): num = jnp.sum(got[:, :, :width] * scale[:, :, None], axis=0)]
  transfers between devices with their start and end apart: 1 -> 0, of which waited for: 1 -> 0; matrix products, arithmetic and copies ran while one was open for 0% -> 0% of each run, Pallas kernels for 0% -> 0%
where the time goes in v1:
time: 53.5 us; the launch traced here: 53.3 us
  blocking collectives  28.9 us (54%)
  matrix products  18.3 us (34%)
  other arithmetic  3.64 us (7%)
  local copies, waits for them, and re-layouts  2.3 us (4%)
    all_to_all x1, blocking collectives, body(): lax.all_to_all(sent.reshape(devices, -1, width + LANES), 'seq', 0, 0)  17.4 us
    all_to_all x1, blocking collectives, body(): lax.all_to_all(jnp.broadcast_to(slot_out, (devices, *slot_out.shape[1:]))...  11.6 us
    dot_general x1, matrix products, body(): jnp.einsum('esf,efd->esd', hidden, w_out, preferred_element_type=jnp.floa...  6.84 us
    dot_general x1, matrix products, body(): logits = jnp.dot(tokens, slot_proj, preferred_element_type=jnp.float32)  5.46 us
    dot_general x1, matrix products, body(): jnp.dot(combine, slot_all.reshape(-1, width), preferred_element_type=jnp....  4.71 us
    reduce_sum x1, other arithmetic, body(): num = jnp.sum(got[:, :, :width] * scale[:, :, None], axis=0)  2.24 us
    dot_general x1, matrix products, body(): lax.dot_general(shifted.astype(jnp.bfloat16), tokens, (((0,), (0,)), ((),...  1.32 us

profile of v1, /device:TPU:1, one launch (start us, length us, event | category | flops | bytes accessed | tf_op | source)
XLA Modules:
  0.0 53.3 jit_solution(14569441415153442758)
XLA Ops:
  0.0 0.0 copy-start
  0.0 0.0 copy-start.1
  0.0 0.9 %copy-done = bf16[1280,64]{0,1:T(8,128)(2,1)S(1)} copy-done((bf16[1280,64]{0,1:T(8,128)(2,1)S(1)}, bf16[1280,64]{0,1:T(8,128)(2,1)}, u32[]{:S(2)}) %copy-start) | copy-done | bytes 163864
  0.9 5.5 %fusion.44 = (f32[2560]{0:T(1024)S(1)}, f32[64]{0:T(128)S(1)}, f32[2560,64]{0,1:T(8,128)S(1)}) fusion(bf16[2560,1280]{1,0:T(8,128)(2,1)} %param.4, bf16[1280,64]{0,1:T(8,128)(2,1)S(1)} %copy-done), kind=kOutput, calls=%fused_computation.58 | convolution fusion | flops 419755456 | bytes 7383296 | tf_op jit(solution)/shard_map/dot_general | solution.py:19
  6.4 0.0 copy-done.1
  6.4 1.3 %convolution_convert_fusion.1 = bf16[64,1280]{1,0:T(8,128)(2,1)S(1)} fusion(bf16[2560,1280]{1,0:T(8,128)(2,1)S(1)} %copy-done.1, f32[2560,64]{0,1:T(8,128)S(1)} %get-tuple-element.17, f32[64]{0:T(128)S(1)} %get-tuple-element.8), kind=kOutput, calls=%fused_computation.5 | convolution fusion | flops 419840000 | bytes 7373056 | tf_op jit(solution)/shard_map/dot_general | solution.py:23
  7.7 0.3 fusion.8
  8.1 0.1 copy.27
  8.2 0.1 concatenate.9
  8.3 0.2 pad_maximum_fusion
  8.4 17.4 %all_to_all.10 = bf16[32,2,1408]{2,1,0:T(2,128)(2,1)S(1)} all-to-all(bf16[32,2,1408]{2,1,0:T(2,128)(2,1)S(1)} %pad_maximum_fusion), channel_id=1, replica_groups=mesh['clip'=4,'seq'=32] {'seq'}, dimensions={0} | all-to-all | bytes 360448 | tf_op jit(solution)/shard_map/all_to_all | solution.py:29
  25.8 1.0 %copy.26 = bf16[32,2,1408]{0,1,2:T(2,128)(2,1)S(1)} copy(bf16[32,2,1408]{2,1,0:T(2,128)(2,1)S(1)} %all_to_all.10) | data formatting | bytes 360448 | tf_op jit(solution)/shard_map/all_to_all | solution.py:29
  26.8 0.5 %convert_element_type.31 = f32[32,2,1408]{0,1,2:T(2,128)S(1)} convert(bf16[32,2,1408]{0,1,2:T(2,128)(2,1)S(1)} %copy.26) | non-fusion elementwise | flops 90112 | bytes 540672 | tf_op jit(solution)/shard_map/convert_element_type | solution.py:29
  27.4 0.1 fusion.45
  27.5 0.2 fusion.36
  27.7 0.1 exponential_bitcast_fusion
  27.8 2.2 %fusion.7 = f32[2,1280]{0,1:T(8,128)S(1)} fusion(f32[32,2,1408]{0,1,2:T(2,128)S(1)} %convert_element_type.31, f32[32,2]{0,1:T(2,128)S(1)} %exponential_bitcast_fusion), kind=kLoop, calls=%fused_computation.8 | loop fusion | flops 161280 | bytes 338176 | tf_op jit(solution)/shard_map/reduce_sum | solution.py:33
  30.0 6.8 %fusion.4 = bf16[2,1280]{1,0:T(2,128)(2,1)S(1)} fusion(bf16[1,2560,1280]{2,1,0:T(8,128)(2,1)} %param.7, bf16[1,1280,2560]{2,1,0:T(8,128)(2,1)} %param.6, f32[2,1280]{0,1:T(8,128)S(1)} %fusion.7, f32[2]{0:T(128)S(1)} %fusion.36), kind=kOutput, calls=%fused_computation.6 | convolution fusion | flops 26268160 | bytes 13122568 | tf_op jit(solution)/shard_map/esf,efd->esd/dot_general | solution.py:39
  36.9 0.1 broadcast_in_dim.2
  37.0 11.6 %all_to_all.11 = bf16[32,2,1280]{2,1,0:T(2,128)(2,1)S(1)} all-to-all(bf16[32,2,1280]{2,1,0:T(2,128)(2,1)S(1)} %broadcast_in_dim.2), channel_id=1, replica_groups=mesh['clip'=4,'seq'=32] {'seq'}, dimensions={0} | all-to-all | bytes 327680 | tf_op jit(solution)/shard_map/all_to_all | solution.py:43
  48.5 0.1 reshape.106
  48.6 4.7 %convolution_convert_fusion = bf16[2560,1280]{1,0:T(8,128)(2,1)} fusion(bf16[64,1280]{1,0:T(8,128)(2,1)S(1)} %reshape.106, f32[2560,64]{0,1:T(8,128)S(1)} %get-tuple-element.17, f32[2560]{0:T(1024)S(1)} %get-tuple-element.5, f32[2560]{0:T(1024)S(1)} %get-tuple-element.7), kind=kOutput, calls=%fused_computation | convolution fusion | flops 423198720 | bytes 7393280 | tf_op jit(solution)/shard_map/dot_general | solution.py:45
  (3 shorter events, 0.1 us)
Async XLA Ops:
  0.0 0.9 %copy-start = (bf16[1280,64]{0,1:T(8,128)(2,1)S(1)}, bf16[1280,64]{0,1:T(8,128)(2,1)}, u32[]{:S(2)}) copy-start(bf16[1280,64]{0,1:T(8,128)(2,1)} %param.5) | copy-start | bytes 491524
  0.0 6.4 %copy-start.1 = (bf16[2560,1280]{1,0:T(8,128)(2,1)S(1)}, bf16[2560,1280]{1,0:T(8,128)(2,1)}, u32[]{:S(2)}) copy-start(bf16[2560,1280]{1,0:T(8,128)(2,1)} %param.4) | copy-start | bytes 19660804

commit v2 on v1

v2 whole, which is shorter than its diff:
```python
import functools

import jax
import jax.numpy as jnp
from jax import lax
from jax.experimental import pallas as pl
from jax.experimental.pallas import tpu as pltpu
from jax.sharding import PartitionSpec as P

SLOTS = 2
LANES = 128
MIB = 1 << 20
DLIM = 20
OUT = jax.ShapeDtypeStruct


def split3(x):
    hi = x.astype(jnp.bfloat16).astype(jnp.float32)
    mid = (x - hi).astype(jnp.bfloat16).astype(jnp.float32)
    return [hi, mid, x - hi - mid]


def dispatch_kernel(chunks, tokens_ref, proj_hbm, sent_ref, logits_ref, held, acc, proj_ref, sem):
    slots, width = proj_ref.shape
    starts = [sum(chunks[:i]) for i in range(len(chunks))]

    def copy(i):
        part = pl.ds(starts[i], chunks[i])
        return pltpu.make_async_copy(tokens_ref.at[part], held.at[part], sem.at[i])

    proj_copy = pltpu.make_async_copy(proj_hbm, proj_ref, sem.at[len(chunks)])
    proj_copy.start()
    for i in range(len(chunks)):
        copy(i).start()
    proj_copy.wait()

    def halves(i):
        rows = chunks[i] // 2
        return [pl.ds(starts[i] + k * rows, rows) for k in range(2)]

    def chunk_logits(i):
        copy(i).wait()
        blocks = []
        for part in halves(i):
            block = lax.dot_general(
                held[part, :], proj_ref[...], (((1,), (1,)), ((), ())), preferred_element_type=jnp.float32
            )
            logits_ref[part, :] = block
            blocks.append(block)
        return blocks

    top = jnp.full((1, slots), -jnp.inf, jnp.float32)
    total = jnp.zeros((1, slots), jnp.float32)
    blocks = chunk_logits(0)
    for i in range(len(chunks)):
        following = chunk_logits(i + 1) if i + 1 < len(chunks) else None
        new_top = top
        for block in blocks:
            new_top = jnp.maximum(new_top, jnp.max(block, axis=0, keepdims=True))
        fade = jnp.exp(top - new_top)
        total = total * fade
        adds = []
        for part, block in zip(halves(i), blocks):
            shifted = jnp.exp(block - new_top)
            total = total + jnp.sum(shifted, axis=0, keepdims=True)
            adds.append(
                lax.dot_general(
                    shifted.astype(jnp.bfloat16), held[part, :], (((0,), (0,)), ((), ())),
                    preferred_element_type=jnp.float32,
                )
            )
        add = adds[0] + adds[1]
        acc[...] = add if i == 0 else acc[...] * fade.reshape(slots, 1) + add
        top, blocks = new_top, following
    lanes = [*split3(top), *split3(total)]
    stats = jnp.concatenate([*lanes, jnp.zeros((LANES - len(lanes), slots), jnp.float32)], axis=0)
    sums = acc[...].astype(jnp.bfloat16)
    stats = stats.T.astype(jnp.bfloat16)
    for k in range(slots // SLOTS):
        sent_ref[k, :, :width] = sums[SLOTS * k : SLOTS * (k + 1), :]
        sent_ref[k, :, width:] = stats[SLOTS * k : SLOTS * (k + 1), :]


def dispatch(tokens, slot_proj, devices):
    count, width = tokens.shape
    slots = slot_proj.shape[1]
    unit = count // 20
    chunks = (4 * unit, 4 * unit, 6 * unit, 6 * unit)
    return pl.pallas_call(
        functools.partial(dispatch_kernel, chunks),
        out_shape=(
            OUT((devices, slots // devices, width + LANES), jnp.bfloat16),
            OUT((count, slots), jnp.float32),
        ),
        in_specs=[pl.BlockSpec(memory_space=pltpu.HBM)] * 2,
        out_specs=(pl.BlockSpec(memory_space=pltpu.VMEM), pl.BlockSpec(memory_space=pltpu.VMEM)),
        scratch_shapes=[
            pltpu.VMEM((count, width), jnp.bfloat16),
            pltpu.VMEM((slots, width), jnp.float32),
            pltpu.VMEM((slots, width), jnp.bfloat16),
            pltpu.SemaphoreType.DMA((len(chunks) + 1,)),
        ],
        compiler_params=pltpu.CompilerParams(vmem_limit_bytes=DLIM * MIB),
        cost_estimate=pl.CostEstimate(flops=4 * count * width * slots, bytes_accessed=2 * count * width, transcendentals=count * slots),
        name="dispatch",
    )(pltpu.with_memory_space_constraint(tokens, pltpu.HBM), pltpu.with_memory_space_constraint(slot_proj.T, pltpu.HBM))


def combine_kernel(logits_ref, combine_ref):
    block = logits_ref[...]
    shifted = jnp.exp(block - jnp.max(block, axis=1, keepdims=True))
    combine_ref[...] = (shifted / jnp.sum(shifted, axis=1, keepdims=True)).astype(combine_ref.dtype)


def combine_weights(logits):
    return pl.pallas_call(
        combine_kernel,
        out_shape=jax.ShapeDtypeStruct(logits.shape, jnp.bfloat16),
        in_specs=[pl.BlockSpec(memory_space=pltpu.VMEM)],
        out_specs=pl.BlockSpec(memory_space=pltpu.VMEM),
        compiler_params=pltpu.CompilerParams(vmem_limit_bytes=16 * MIB),
        cost_estimate=pl.CostEstimate(flops=5 * logits.size, bytes_accessed=6 * logits.size, transcendentals=logits.size),
        name="combine_weights",
    )(logits)


def expert_kernel(got_ref, w_in_ref, w_out_ref, out_ref, hidden_ref):
    width = w_in_ref.shape[1]
    devices = got_ref.shape[0]
    got = got_ref[...].astype(jnp.float32)
    stats = got[:, :, width:]
    maxes = stats[:, :, 0:1] + stats[:, :, 1:2] + stats[:, :, 2:3]
    totals = stats[:, :, 3:4] + stats[:, :, 4:5] + stats[:, :, 5:6]
    scale = jnp.exp(maxes - jnp.max(maxes, axis=0, keepdims=True))
    num = jnp.sum(got[:, :, :width] * scale, axis=0)
    slot_in = (num / jnp.sum(totals * scale, axis=0)).astype(jnp.bfloat16)
    hidden = jnp.dot(slot_in, w_in_ref[0], preferred_element_type=jnp.float32)
    hidden = jax.nn.gelu(hidden).astype(jnp.bfloat16)
    out = jnp.dot(hidden, w_out_ref[0], preferred_element_type=jnp.float32).astype(jnp.bfloat16)
    for k in range(devices):
        out_ref[k] = out


def expert(got, w_in, w_out):
    devices, slots, _ = got.shape
    return pl.pallas_call(
        expert_kernel,
        out_shape=jax.ShapeDtypeStruct((devices, slots, w_in.shape[1]), jnp.bfloat16),
        in_specs=[pl.BlockSpec(memory_space=pltpu.VMEM)] * 3,
        out_specs=pl.BlockSpec(memory_space=pltpu.VMEM),
        scratch_shapes=[pltpu.VMEM((slots, w_in.shape[2]), jnp.float32)],
        compiler_params=pltpu.CompilerParams(vmem_limit_bytes=WLIM * MIB),
        cost_estimate=pl.CostEstimate(flops=4 * slots * w_in.size, bytes_accessed=4 * w_in.size, transcendentals=slots * w_in.shape[2]),
        name="expert",
    )(got, WC(w_in), WC(w_out))


def mix_kernel(blocks, combine_ref, slot_ref, mixed_ref, slot_all, held, sem):
    rows = combine_ref.shape[0] // blocks
    for k in range(slot_ref.shape[0]):
        slot_all[SLOTS * k : SLOTS * (k + 1), :] = slot_ref[k]
    for i in range(blocks):
        part = pl.ds(i * rows, rows)
        held[part, :] = jnp.dot(
            combine_ref[part, :], slot_all[...], preferred_element_type=jnp.float32
        ).astype(jnp.bfloat16)
        pltpu.make_async_copy(held.at[part], mixed_ref.at[part], sem.at[i]).start()
    for i in range(blocks):
        part = pl.ds(i * rows, rows)
        pltpu.make_async_copy(held.at[part], mixed_ref.at[part], sem.at[i]).wait()


def mix(combine, slot_all, blocks=10):
    count, slots = combine.shape
    width = slot_all.shape[2]
    return pl.pallas_call(
        functools.partial(mix_kernel, blocks),
        out_shape=jax.ShapeDtypeStruct((count, width), jnp.bfloat16),
        in_specs=[pl.BlockSpec(memory_space=pltpu.VMEM)] * 2,
        out_specs=pl.BlockSpec(memory_space=pl.ANY),
        scratch_shapes=[
            pltpu.VMEM((slots, width), jnp.bfloat16),
            pltpu.VMEM((count, width), jnp.bfloat16),
            pltpu.SemaphoreType.DMA((blocks,)),
        ],
        compiler_params=pltpu.CompilerParams(vmem_limit_bytes=24 * MIB),
        cost_estimate=pl.CostEstimate(flops=2 * count * width * slots, bytes_accessed=2 * count * width, transcendentals=0),
        name="mix",
    )(combine, slot_all)


WLIM = 16
def WC(x):
    return pltpu.with_memory_space_constraint(x, pltpu.VMEM)


def body(tokens, slot_proj, w_in, w_out):
    devices = lax.axis_size("seq")
    sent, logits = dispatch(tokens, slot_proj, devices)
    got = lax.all_to_all(sent, "seq", 0, 0)
    combine = combine_weights(logits)
    slot_out = expert(got, w_in, w_out)
    slot_all = lax.all_to_all(slot_out, "seq", 0, 0)
    return mix(combine, slot_all)


def solution(mesh):
    return jax.shard_map(
        body,
        mesh=mesh,
        in_specs=(P(("clip", "seq"), None), P(), P("seq", None, None), P("seq", None, None)),
        out_specs=P(("clip", "seq"), None),
        check_vma=False,
    )
```

time: 53.5 us -> 43.6 us (0.81)
  matrix products: 18.3 us -> 0 us
  Pallas kernels: 0 us -> 11.9 us
  blocking collectives: 28.9 us -> 17.4 us
  waiting for transfers between devices: 0 us -> 7.35 us
  starting transfers between devices: 0 us -> 3.83 us
  other arithmetic: 3.64 us -> 0 us
  local copies, waits for them, and re-layouts: 2.3 us -> 2.86 us
    dot_general x4 -> x0, matrix products: 18.3 us -> none  [the longest x1 6.84 us: body(): jnp.einsum('esf,efd->esd', hidden, w_out, preferred_element_type=jnp.floa...]
    pallas_call x0 -> x4, Pallas kernels: none -> 11.9 us  [the longest x1 4.94 us: dispatch(): pl.pallas_call(functools.partial(dispatch_kernel, chunks), out_shape=(OUT...]
    all_to_all x2 -> x1, blocking collectives: 28.9 us -> 17.4 us  [body(): got = lax.all_to_all(sent, 'seq', 0, 0)]
    all_to_all x0 -> x1, waiting for transfers between devices: none -> 7.35 us  [body(): slot_all = lax.all_to_all(slot_out, 'seq', 0, 0)]
    all_to_all x0 -> x1, starting transfers between devices: none -> 3.83 us  [body(): slot_all = lax.all_to_all(slot_out, 'seq', 0, 0)]
    reduce_sum x3 -> x0, other arithmetic: 2.73 us -> none  [the longest x1 2.24 us: body(): num = jnp.sum(got[:, :, :width] * scale[:, :, None], axis=0)]
    unnamed x5 -> x4, local copies, waits for them, and re-layouts: 1.03 us -> 2.86 us
    all_to_all x1 -> x0, local copies, waits for them, and re-layouts: 1 us -> none  [body(): lax.all_to_all(sent.reshape(devices, -1, width + LANES), 'seq', 0, 0)]
  transfers between devices with their start and end apart: 0 -> 1, of which waited for: 0 -> 1; matrix products, arithmetic and copies ran while one was open for 0% -> 0% of each run, Pallas kernels for 0% -> 2%
where the time goes in v2:
time: 43.6 us; the launch traced here: 43.3 us
  blocking collectives  17.4 us (40%)
  Pallas kernels  11.9 us (27%)
  waiting for transfers between devices  7.35 us (17%)
  starting transfers between devices  3.83 us (9%)
  local copies, waits for them, and re-layouts  2.86 us (7%)
    all_to_all x1, blocking collectives, body(): got = lax.all_to_all(sent, 'seq', 0, 0)  17.4 us
    all_to_all x1, waiting for transfers between devices, body(): slot_all = lax.all_to_all(slot_out, 'seq', 0, 0)  7.35 us
    pallas_call x1, Pallas kernels, dispatch(): pl.pallas_call(functools.partial(dispatch_kernel, chunks), out_shape=(OUT...  4.94 us
    all_to_all x1, starting transfers between devices, body(): slot_all = lax.all_to_all(slot_out, 'seq', 0, 0)  3.83 us
    pallas_call x1, Pallas kernels, mix(): pl.pallas_call(functools.partial(mix_kernel, blocks), out_shape=jax.Shape...  3.22 us
    pallas_call x1, Pallas kernels, expert(): pl.pallas_call(expert_kernel, out_shape=jax.ShapeDtypeStruct((devices, sl...  2.95 us
    unnamed x4, local copies, waits for them, and re-layouts  2.86 us
  transfers between devices with their start and end apart: 1, of which 1 were waited for; matrix products, arithmetic and copies ran while one was open for 0% of the time, Pallas kernels for 2%

profile of v2, /device:TPU:1, one launch (start us, length us, event | category | flops | bytes accessed | tf_op | source)
XLA Modules:
  0.0 43.3 jit_solution(17804782945946814025)
XLA Ops:
  0.0 0.0 copy-start
  0.0 4.9 %dispatch.1 = (bf16[32,2,1408]{2,1,0:T(2,128)(2,1)S(1)}, f32[2560,64]{1,0:T(8,128)S(1)}) custom-call(bf16[2560,1280]{1,0:T(8,128)(2,1)} %tokens_ref.1, bf16[64,1280]{1,0:T(8,128)(2,1)} %bitcast.1), custom_call_target="tpu_custom_call" | custom-call | flops 838860800 | bytes 6553600 | tf_op jit(solution)/shard_map/dispatch/pallas_call | solution.py:89
  5.0 17.4 %all_to_all.10.got_ref = bf16[32,2,1408]{2,1,0:T(2,128)(2,1)S(1)} all-to-all(bf16[32,2,1408]{2,1,0:T(2,128)(2,1)S(1)} %get-tuple-element.8), channel_id=1, replica_groups=mesh['clip'=4,'seq'=32] {'seq'}, dimensions={0} | all-to-all | bytes 360448 | tf_op jit(solution)/shard_map/all_to_all | solution.py:200
  22.3 0.0 copy-done
  22.3 0.0 copy-start.1
  22.3 2.9 %copy-done.1 = bf16[1,2560,1280]{2,1,0:T(8,128)(2,1)S(1)} copy-done((bf16[1,2560,1280]{2,1,0:T(8,128)(2,1)S(1)}, bf16[1,2560,1280]{2,1,0:T(8,128)(2,1)}, u32[]{:S(2)}) %copy-start.1) | copy-done | bytes 6553624
  25.2 2.9 %expert.1 = bf16[32,2,1280]{2,1,0:T(2,128)(2,1)} custom-call(bf16[32,2,1408]{2,1,0:T(2,128)(2,1)S(1)} %all_to_all.10.got_ref, bf16[1,1280,2560]{2,1,0:T(8,128)(2,1)S(1)} %copy-done, bf16[1,2560,1280]{2,1,0:T(8,128)(2,1)S(1)} %copy-done.1), custom_call_target="tpu_custom_call" | custom-call | flops 26214400 | bytes 13107200 | tf_op jit(solution)/shard_map/expert/pallas_call | solution.py:146
  28.1 3.8 %all-to-all-start.1 = ((bf16[32,2,1280]{2,1,0:T(2,128)(2,1)}), bf16[32,2,1280]{2,1,0:T(2,128)(2,1)S(1)}, u32[]{:S(2)}, u32[]{:S(2)}) async-start(bf16[32,2,1280]{2,1,0:T(2,128)(2,1)} %expert.1), calls=%async_computation.1 | async-start | bytes 327680 | tf_op jit(solution)/shard_map/all_to_all | solution.py:203
  32.0 0.8 %combine_weights.1.combine_ref = bf16[2560,64]{1,0:T(8,128)(2,1)S(1)} custom-call(f32[2560,64]{1,0:T(8,128)S(1)} %get-tuple-element.7.logits_ref), custom_call_target="tpu_custom_call" | custom-call | flops 819200 | bytes 983040 | tf_op jit(solution)/shard_map/combine_weights/pallas_call | solution.py:116
  32.8 7.4 %all-to-all-done.1.slot_ref = bf16[32,2,1280]{2,1,0:T(2,128)(2,1)S(1)} async-done(((bf16[32,2,1280]{2,1,0:T(2,128)(2,1)}), bf16[32,2,1280]{2,1,0:T(2,128)(2,1)S(1)}, u32[]{:S(2)}, u32[]{:S(2)}) %all-to-all-start.1) | async-done | bytes 163872 | tf_op jit(solution)/shard_map/all_to_all | solution.py:203
  40.1 3.2 %mix.1 = bf16[2560,1280]{1,0:T(8,128)(2,1)} custom-call(bf16[2560,64]{1,0:T(8,128)(2,1)S(1)} %combine_weights.1.combine_ref, bf16[32,2,1280]{2,1,0:T(2,128)(2,1)S(1)} %all-to-all-done.1.slot_ref), custom_call_target="tpu_custom_call" | custom-call | flops 419430400 | bytes 6553600 | tf_op jit(solution)/shard_map/mix/pallas_call | solution.py:176
Async XLA Ops:
  0.0 22.3 %copy-start = (bf16[1,1280,2560]{2,1,0:T(8,128)(2,1)S(1)}, bf16[1,1280,2560]{2,1,0:T(8,128)(2,1)}, u32[]{:S(2)}) copy-start(bf16[1,1280,2560]{2,1,0:T(8,128)(2,1)} %w_in_ref.1) | copy-start | bytes 19660804
  22.3 2.9 %copy-start.1 = (bf16[1,2560,1280]{2,1,0:T(8,128)(2,1)S(1)}, bf16[1,2560,1280]{2,1,0:T(8,128)(2,1)}, u32[]{:S(2)}) copy-start(bf16[1,2560,1280]{2,1,0:T(8,128)(2,1)} %w_out_ref.1) | copy-start | bytes 19660804
  28.1 12.0 %all-to-all-start.1 = ((bf16[32,2,1280]{2,1,0:T(2,128)(2,1)}), bf16[32,2,1280]{2,1,0:T(2,128)(2,1)S(1)}, u32[]{:S(2)}, u32[]{:S(2)}) async-start(bf16[32,2,1280]{2,1,0:T(2,128)(2,1)} %expert.1), calls=%async_computation.1 | async-start | bytes 327680 | tf_op jit(solution)/shard_map/all_to_all | solution.py:203

commit v3 on v2

--- a/solution.py
+++ b/solution.py
@@ -101,7 +101,7 @@
             pltpu.SemaphoreType.DMA((len(chunks) + 1,)),
         ],
         compiler_params=pltpu.CompilerParams(vmem_limit_bytes=DLIM * MIB),
-        cost_estimate=pl.CostEstimate(flops=4 * count * width * slots, bytes_accessed=2 * count * width, transcendentals=count * slots),
+        cost_estimate=pl.CostEstimate(flops=32 * count * width * slots, bytes_accessed=2 * count * width, transcendentals=count * slots),
         name="dispatch",
     )(pltpu.with_memory_space_constraint(tokens, pltpu.HBM), pltpu.with_memory_space_constraint(slot_proj.T, pltpu.HBM))
 

time: 43.6 us -> 40.9 us (0.938)
  local copies, waits for them, and re-layouts: 2.86 us -> 0.01 us
    unnamed x4, local copies, waits for them, and re-layouts: 2.86 us -> 0.01 us
where the time goes in v3:
time: 40.9 us; the launch traced here: 40.7 us
  blocking collectives  17.7 us (43%)
  Pallas kernels  11.9 us (29%)
  waiting for transfers between devices  7.35 us (18%)
  starting transfers between devices  3.83 us (9%)
    all_to_all x1, blocking collectives, body(): got = lax.all_to_all(sent, 'seq', 0, 0)  17.7 us
    all_to_all x1, waiting for transfers between devices, body(): slot_all = lax.all_to_all(slot_out, 'seq', 0, 0)  7.35 us
    pallas_call x1, Pallas kernels, dispatch(): pl.pallas_call(functools.partial(dispatch_kernel, chunks), out_shape=(OUT...  4.93 us
    all_to_all x1, starting transfers between devices, body(): slot_all = lax.all_to_all(slot_out, 'seq', 0, 0)  3.83 us
    pallas_call x1, Pallas kernels, mix(): pl.pallas_call(functools.partial(mix_kernel, blocks), out_shape=jax.Shape...  3.22 us
    pallas_call x1, Pallas kernels, expert(): pl.pallas_call(expert_kernel, out_shape=jax.ShapeDtypeStruct((devices, sl...  2.95 us
  transfers between devices with their start and end apart: 1, of which 1 were waited for; matrix products, arithmetic and copies ran while one was open for 0% of the time, Pallas kernels for 2%

profile of v3, /device:TPU:1, one launch (start us, length us, event | category | flops | bytes accessed | tf_op | source)
XLA Modules:
  0.0 40.7 jit_solution(17795463002966607181)
XLA Ops:
  0.0 0.0 copy-start
  0.0 0.0 copy-start.1
  0.0 4.9 %dispatch.1 = (bf16[32,2,1408]{2,1,0:T(2,128)(2,1)S(1)}, f32[2560,64]{1,0:T(8,128)S(1)}) custom-call(bf16[2560,1280]{1,0:T(8,128)(2,1)} %tokens_ref.1, bf16[64,1280]{1,0:T(8,128)(2,1)} %bitcast.1), custom_call_target="tpu_custom_call" | custom-call | flops 6710886400 | bytes 6553600 | tf_op jit(solution)/shard_map/dispatch/pallas_call | solution.py:89
  4.9 17.7 %all_to_all.10.got_ref = bf16[32,2,1408]{2,1,0:T(2,128)(2,1)S(1)} all-to-all(bf16[32,2,1408]{2,1,0:T(2,128)(2,1)S(1)} %get-tuple-element.8), channel_id=1, replica_groups=mesh['clip'=4,'seq'=32] {'seq'}, dimensions={0} | all-to-all | bytes 360448 | tf_op jit(solution)/shard_map/all_to_all | solution.py:200
  22.6 0.0 copy-done
  22.6 0.0 copy-done.1
  22.6 2.9 %expert.1 = bf16[32,2,1280]{2,1,0:T(2,128)(2,1)} custom-call(bf16[32,2,1408]{2,1,0:T(2,128)(2,1)S(1)} %all_to_all.10.got_ref, bf16[1,1280,2560]{2,1,0:T(8,128)(2,1)S(1)} %copy-done, bf16[1,2560,1280]{2,1,0:T(8,128)(2,1)S(1)} %copy-done.1), custom_call_target="tpu_custom_call" | custom-call | flops 26214400 | bytes 13107200 | tf_op jit(solution)/shard_map/expert/pallas_call | solution.py:146
  25.6 3.8 %all-to-all-start.1 = ((bf16[32,2,1280]{2,1,0:T(2,128)(2,1)}), bf16[32,2,1280]{2,1,0:T(2,128)(2,1)S(1)}, u32[]{:S(2)}, u32[]{:S(2)}) async-start(bf16[32,2,1280]{2,1,0:T(2,128)(2,1)} %expert.1), calls=%async_computation.1 | async-start | bytes 327680 | tf_op jit(solution)/shard_map/all_to_all | solution.py:203
  29.4 0.8 %combine_weights.1.combine_ref = bf16[2560,64]{1,0:T(8,128)(2,1)S(1)} custom-call(f32[2560,64]{1,0:T(8,128)S(1)} %get-tuple-element.7.logits_ref), custom_call_target="tpu_custom_call" | custom-call | flops 819200 | bytes 983040 | tf_op jit(solution)/shard_map/combine_weights/pallas_call | solution.py:116
  30.2 7.4 %all-to-all-done.1.slot_ref = bf16[32,2,1280]{2,1,0:T(2,128)(2,1)S(1)} async-done(((bf16[32,2,1280]{2,1,0:T(2,128)(2,1)}), bf16[32,2,1280]{2,1,0:T(2,128)(2,1)S(1)}, u32[]{:S(2)}, u32[]{:S(2)}) %all-to-all-start.1) | async-done | bytes 163872 | tf_op jit(solution)/shard_map/all_to_all | solution.py:203
  37.5 3.2 %mix.1 = bf16[2560,1280]{1,0:T(8,128)(2,1)} custom-call(bf16[2560,64]{1,0:T(8,128)(2,1)S(1)} %combine_weights.1.combine_ref, bf16[32,2,1280]{2,1,0:T(2,128)(2,1)S(1)} %all-to-all-done.1.slot_ref), custom_call_target="tpu_custom_call" | custom-call | flops 419430400 | bytes 6553600 | tf_op jit(solution)/shard_map/mix/pallas_call | solution.py:176
Async XLA Ops:
  0.0 22.6 %copy-start = (bf16[1,1280,2560]{2,1,0:T(8,128)(2,1)S(1)}, bf16[1,1280,2560]{2,1,0:T(8,128)(2,1)}, u32[]{:S(2)}) copy-start(bf16[1,1280,2560]{2,1,0:T(8,128)(2,1)} %w_in_ref.1) | copy-start | bytes 19660804
  0.0 22.6 %copy-start.1 = (bf16[1,2560,1280]{2,1,0:T(8,128)(2,1)S(1)}, bf16[1,2560,1280]{2,1,0:T(8,128)(2,1)}, u32[]{:S(2)}) copy-start(bf16[1,2560,1280]{2,1,0:T(8,128)(2,1)} %w_out_ref.1) | copy-start | bytes 19660804
  25.6 12.0 %all-to-all-start.1 = ((bf16[32,2,1280]{2,1,0:T(2,128)(2,1)}), bf16[32,2,1280]{2,1,0:T(2,128)(2,1)S(1)}, u32[]{:S(2)}, u32[]{:S(2)}) async-start(bf16[32,2,1280]{2,1,0:T(2,128)(2,1)} %expert.1), calls=%async_computation.1 | async-start | bytes 327680 | tf_op jit(solution)/shard_map/all_to_all | solution.py:203

commit v4 on v3

--- a/solution.py
+++ b/solution.py
@@ -10,6 +10,8 @@
 SLOTS = 2
 LANES = 128
 MIB = 1 << 20
+ORDER1 = [31, 30, 29, 28, 27, 26, 25, 24, 23, 22, 21, 20, 19, 18, 17, 16, 15, 14, 13, 12, 11, 10, 9, 8, 7, 6, 5, 4, 3, 2, 1, 0]
+ORDER2 = [21, 20, 29, 28, 23, 22, 19, 18, 13, 12, 31, 30, 27, 26, 17, 16, 15, 14, 11, 10, 5, 4, 25, 24, 9, 8, 7, 6, 3, 2, 1, 0]
 DLIM = 20
 OUT = jax.ShapeDtypeStruct
 
@@ -76,9 +78,10 @@
     stats = jnp.concatenate([*lanes, jnp.zeros((LANES - len(lanes), slots), jnp.float32)], axis=0)
     sums = acc[...].astype(jnp.bfloat16)
     stats = stats.T.astype(jnp.bfloat16)
-    for k in range(slots // SLOTS):
-        sent_ref[k, :, :width] = sums[SLOTS * k : SLOTS * (k + 1), :]
-        sent_ref[k, :, width:] = stats[SLOTS * k : SLOTS * (k + 1), :]
+    for j in range(slots // SLOTS):
+        k = ORDER1[j]
+        sent_ref[j, :, :width] = sums[SLOTS * k : SLOTS * (k + 1), :]
+        sent_ref[j, :, width:] = stats[SLOTS * k : SLOTS * (k + 1), :]
 
 
 def dispatch(tokens, slot_proj, devices):
@@ -106,25 +109,14 @@
     )(pltpu.with_memory_space_constraint(tokens, pltpu.HBM), pltpu.with_memory_space_constraint(slot_proj.T, pltpu.HBM))
 
 
-def combine_kernel(logits_ref, combine_ref):
-    block = logits_ref[...]
-    shifted = jnp.exp(block - jnp.max(block, axis=1, keepdims=True))
-    combine_ref[...] = (shifted / jnp.sum(shifted, axis=1, keepdims=True)).astype(combine_ref.dtype)
-
-
-def combine_weights(logits):
-    return pl.pallas_call(
-        combine_kernel,
-        out_shape=jax.ShapeDtypeStruct(logits.shape, jnp.bfloat16),
-        in_specs=[pl.BlockSpec(memory_space=pltpu.VMEM)],
-        out_specs=pl.BlockSpec(memory_space=pltpu.VMEM),
-        compiler_params=pltpu.CompilerParams(vmem_limit_bytes=16 * MIB),
-        cost_estimate=pl.CostEstimate(flops=5 * logits.size, bytes_accessed=6 * logits.size, transcendentals=logits.size),
-        name="combine_weights",
-    )(logits)
-
-
-def expert_kernel(got_ref, w_in_ref, w_out_ref, out_ref, hidden_ref):
+def halves_dot(rows, weights_ref):
+    half = weights_ref.shape[2] // 2
+    return [
+        jnp.dot(rows, weights_ref[0, :, k * half : (k + 1) * half], preferred_element_type=jnp.float32) for k in range(2)
+    ]
+
+
+def expert_kernel(got_ref, w_in_ref, w_out_ref, out_ref):
     width = w_in_ref.shape[1]
     devices = got_ref.shape[0]
     got = got_ref[...].astype(jnp.float32)
@@ -134,9 +126,8 @@
     scale = jnp.exp(maxes - jnp.max(maxes, axis=0, keepdims=True))
     num = jnp.sum(got[:, :, :width] * scale, axis=0)
     slot_in = (num / jnp.sum(totals * scale, axis=0)).astype(jnp.bfloat16)
-    hidden = jnp.dot(slot_in, w_in_ref[0], preferred_element_type=jnp.float32)
-    hidden = jax.nn.gelu(hidden).astype(jnp.bfloat16)
-    out = jnp.dot(hidden, w_out_ref[0], preferred_element_type=jnp.float32).astype(jnp.bfloat16)
+    hidden = jnp.concatenate([jax.nn.gelu(h).astype(jnp.bfloat16) for h in halves_dot(slot_in, w_in_ref)], axis=1)
+    out = jnp.concatenate([o.astype(jnp.bfloat16) for o in halves_dot(hidden, w_out_ref)], axis=1)
     for k in range(devices):
         out_ref[k] = out
 
@@ -148,45 +139,51 @@
         out_shape=jax.ShapeDtypeStruct((devices, slots, w_in.shape[1]), jnp.bfloat16),
         in_specs=[pl.BlockSpec(memory_space=pltpu.VMEM)] * 3,
         out_specs=pl.BlockSpec(memory_space=pltpu.VMEM),
-        scratch_shapes=[pltpu.VMEM((slots, w_in.shape[2]), jnp.float32)],
         compiler_params=pltpu.CompilerParams(vmem_limit_bytes=WLIM * MIB),
         cost_estimate=pl.CostEstimate(flops=4 * slots * w_in.size, bytes_accessed=4 * w_in.size, transcendentals=slots * w_in.shape[2]),
         name="expert",
     )(got, WC(w_in), WC(w_out))
 
 
-def mix_kernel(blocks, combine_ref, slot_ref, mixed_ref, slot_all, held, sem):
-    rows = combine_ref.shape[0] // blocks
+def mix_kernel(chunks, logits_ref, slot_ref, mixed_ref, slot_all, held, sem):
     for k in range(slot_ref.shape[0]):
-        slot_all[SLOTS * k : SLOTS * (k + 1), :] = slot_ref[k]
-    for i in range(blocks):
-        part = pl.ds(i * rows, rows)
-        held[part, :] = jnp.dot(
-            combine_ref[part, :], slot_all[...], preferred_element_type=jnp.float32
-        ).astype(jnp.bfloat16)
-        pltpu.make_async_copy(held.at[part], mixed_ref.at[part], sem.at[i]).start()
-    for i in range(blocks):
-        part = pl.ds(i * rows, rows)
-        pltpu.make_async_copy(held.at[part], mixed_ref.at[part], sem.at[i]).wait()
-
-
-def mix(combine, slot_all, blocks=10):
-    count, slots = combine.shape
+        slot_all[SLOTS * ORDER2[k] : SLOTS * (ORDER2[k] + 1), :] = slot_ref[k]
+    starts = [sum(chunks[:i]) for i in range(len(chunks))]
+
+    def copy(i):
+        part = pl.ds(starts[i], chunks[i])
+        return pltpu.make_async_copy(held.at[part], mixed_ref.at[part], sem.at[i])
+
+    for i in range(len(chunks)):
+        rows = chunks[i] // 2
+        for part in [pl.ds(starts[i] + k * rows, rows) for k in range(2)]:
+            block = logits_ref[part, :]
+            shifted = jnp.exp(block - jnp.max(block, axis=1, keepdims=True))
+            combine = (shifted / jnp.sum(shifted, axis=1, keepdims=True)).astype(jnp.bfloat16)
+            held[part, :] = jnp.dot(combine, slot_all[...], preferred_element_type=jnp.float32).astype(jnp.bfloat16)
+        copy(i).start()
+    for i in range(len(chunks)):
+        copy(i).wait()
+
+
+def mix(logits, slot_all):
+    count, slots = logits.shape
     width = slot_all.shape[2]
+    chunks = (count // 10,) * 10
     return pl.pallas_call(
-        functools.partial(mix_kernel, blocks),
+        functools.partial(mix_kernel, chunks),
         out_shape=jax.ShapeDtypeStruct((count, width), jnp.bfloat16),
         in_specs=[pl.BlockSpec(memory_space=pltpu.VMEM)] * 2,
         out_specs=pl.BlockSpec(memory_space=pl.ANY),
         scratch_shapes=[
             pltpu.VMEM((slots, width), jnp.bfloat16),
             pltpu.VMEM((count, width), jnp.bfloat16),
-            pltpu.SemaphoreType.DMA((blocks,)),
+            pltpu.SemaphoreType.DMA((len(chunks),)),
         ],
         compiler_params=pltpu.CompilerParams(vmem_limit_bytes=24 * MIB),
-        cost_estimate=pl.CostEstimate(flops=2 * count * width * slots, bytes_accessed=2 * count * width, transcendentals=0),
+        cost_estimate=pl.CostEstimate(flops=2 * count * width * slots, bytes_accessed=2 * count * width, transcendentals=count * slots),
         name="mix",
-    )(combine, slot_all)
+    )(logits, slot_all)
 
 
 WLIM = 16
@@ -197,11 +194,10 @@
 def body(tokens, slot_proj, w_in, w_out):
     devices = lax.axis_size("seq")
     sent, logits = dispatch(tokens, slot_proj, devices)
-    got = lax.all_to_all(sent, "seq", 0, 0)
-    combine = combine_weights(logits)
+    got = lax.all_to_all(sent, "seq", 0, 0, axis_index_groups=[list(ORDER1)])
     slot_out = expert(got, w_in, w_out)
-    slot_all = lax.all_to_all(slot_out, "seq", 0, 0)
-    return mix(combine, slot_all)
+    slot_all = lax.all_to_all(slot_out, "seq", 0, 0, axis_index_groups=[list(ORDER2)])
+    return mix(logits, slot_all)
 
 
 def solution(mesh):

time: 40.9 us -> 35.6 us (0.87)
  waiting for transfers between devices: 7.35 us -> 0 us
  blocking collectives: 17.7 us -> 24.9 us
  starting transfers between devices: 3.83 us -> 0 us
  Pallas kernels: 11.9 us -> 10.5 us
    all_to_all x1 -> x0, waiting for transfers between devices: 7.35 us -> none  [body(): slot_all = lax.all_to_all(slot_out, 'seq', 0, 0)]
    all_to_all x1 -> x2, blocking collectives: 17.7 us -> 24.9 us  [the longest x1 14.4 us: body(): got = lax.all_to_all(sent, 'seq', 0, 0, axis_index_groups=[list(ORDER1)])]
    all_to_all x1 -> x0, starting transfers between devices: 3.83 us -> none  [body(): slot_all = lax.all_to_all(slot_out, 'seq', 0, 0)]
    pallas_call x1, Pallas kernels: 2.95 us -> 2.15 us  [expert(): pl.pallas_call(expert_kernel, out_shape=jax.ShapeDtypeStruct((devices, sl...]
    pallas_call x2 -> x1, Pallas kernels: 3.97 us -> 3.43 us  [mix(): pl.pallas_call(functools.partial(mix_kernel, chunks), out_shape=jax.Shape...]
  transfers between devices with their start and end apart: 1 -> 0, of which waited for: 1 -> 0; matrix products, arithmetic and copies ran while one was open for 0% -> 0% of each run, Pallas kernels for 2% -> 0%
where the time goes in v4:
time: 35.6 us; the launch traced here: 35.4 us
  blocking collectives  24.9 us (70%)
  Pallas kernels  10.5 us (29%)
    all_to_all x1, blocking collectives, body(): got = lax.all_to_all(sent, 'seq', 0, 0, axis_index_groups=[list(ORDER1)])  14.4 us
    all_to_all x1, blocking collectives, body(): lax.all_to_all(slot_out, 'seq', 0, 0, axis_index_groups=[list(ORDER2)])  10.5 us
    pallas_call x1, Pallas kernels, dispatch(): pl.pallas_call(functools.partial(dispatch_kernel, chunks), out_shape=(OUT...  4.93 us
    pallas_call x1, Pallas kernels, mix(): pl.pallas_call(functools.partial(mix_kernel, chunks), out_shape=jax.Shape...  3.43 us
    pallas_call x1, Pallas kernels, expert(): pl.pallas_call(expert_kernel, out_shape=jax.ShapeDtypeStruct((devices, sl...  2.15 us

profile of v4, /device:TPU:1, one launch (start us, length us, event | category | flops | bytes accessed | tf_op | source)
XLA Modules:
  0.0 35.4 jit_solution(3096148032324558622)
XLA Ops:
  0.0 0.0 copy-start
  0.0 0.0 copy-start.1
  0.0 4.9 %dispatch.1 = (bf16[32,2,1408]{2,1,0:T(2,128)(2,1)S(1)}, f32[2560,64]{1,0:T(8,128)S(1)}) custom-call(bf16[2560,1280]{1,0:T(8,128)(2,1)} %tokens_ref.1, bf16[64,1280]{1,0:T(8,128)(2,1)} %bitcast.1), custom_call_target="tpu_custom_call" | custom-call | flops 6710886400 | bytes 6553600 | tf_op jit(solution)/shard_map/dispatch/pallas_call | solution.py:92
  4.9 14.4 %all_to_all.10.got_ref = bf16[32,2,1408]{2,1,0:T(2,128)(2,1)S(1)} all-to-all(bf16[32,2,1408]{2,1,0:T(2,128)(2,1)S(1)} %get-tuple-element.8), channel_id=1, replica_groups={{31,30,29,28,27,26,25,24,23,22,21,20,19,18,17,16,15,14,13,12,11,10,9,8,..., dimensions={0} | all-to-all | bytes 360448 | tf_op jit(solution)/shard_map/all_to_all | solution.py:197
  19.3 0.0 copy-done
  19.3 0.0 copy-done.1
  19.3 2.1 %expert.1 = bf16[32,2,1280]{2,1,0:T(2,128)(2,1)S(1)} custom-call(bf16[32,2,1408]{2,1,0:T(2,128)(2,1)S(1)} %all_to_all.10.got_ref, bf16[1,1280,2560]{2,1,0:T(8,128)(2,1)S(1)} %copy-done, bf16[1,2560,1280]{2,1,0:T(8,128)(2,1)S(1)} %copy-done.1), custom_call_target="tpu_custom_call" | custom-call | flops 26214400 | bytes 13107200 | tf_op jit(solution)/shard_map/expert/pallas_call | solution.py:137
  21.5 10.5 %all_to_all.11.slot_ref = bf16[32,2,1280]{2,1,0:T(2,128)(2,1)S(1)} all-to-all(bf16[32,2,1280]{2,1,0:T(2,128)(2,1)S(1)} %expert.1), channel_id=1, replica_groups={{21,20,29,28,23,22,19,18,13,12,31,30,27,26,17,16,15,14,11,10,5,4,25,24,..., dimensions={0} | all-to-all | bytes 327680 | tf_op jit(solution)/shard_map/all_to_all | solution.py:199
  32.0 3.4 %mix.1 = bf16[2560,1280]{1,0:T(8,128)(2,1)} custom-call(f32[2560,64]{1,0:T(8,128)S(1)} %get-tuple-element.7.logits_ref, bf16[32,2,1280]{2,1,0:T(2,128)(2,1)S(1)} %all_to_all.11.slot_ref), custom_call_target="tpu_custom_call" | custom-call | flops 419430400 | bytes 6553600 | tf_op jit(solution)/shard_map/mix/pallas_call | solution.py:173
Async XLA Ops:
  0.0 19.3 %copy-start = (bf16[1,1280,2560]{2,1,0:T(8,128)(2,1)S(1)}, bf16[1,1280,2560]{2,1,0:T(8,128)(2,1)}, u32[]{:S(2)}) copy-start(bf16[1,1280,2560]{2,1,0:T(8,128)(2,1)} %w_in_ref.1) | copy-start | bytes 19660804
  0.0 19.3 %copy-start.1 = (bf16[1,2560,1280]{2,1,0:T(8,128)(2,1)S(1)}, bf16[1,2560,1280]{2,1,0:T(8,128)(2,1)}, u32[]{:S(2)}) copy-start(bf16[1,2560,1280]{2,1,0:T(8,128)(2,1)} %w_out_ref.1) | copy-start | bytes 19660804

commit v5 on v4

--- a/solution.py
+++ b/solution.py
@@ -10,7 +10,7 @@
 SLOTS = 2
 LANES = 128
 MIB = 1 << 20
-ORDER1 = [31, 30, 29, 28, 27, 26, 25, 24, 23, 22, 21, 20, 19, 18, 17, 16, 15, 14, 13, 12, 11, 10, 9, 8, 7, 6, 5, 4, 3, 2, 1, 0]
+ORDER1 = [23, 22, 21, 20, 19, 18, 17, 16, 15, 14, 13, 12, 11, 10, 9, 8, 7, 6, 5, 4, 3, 2, 1, 0, 31, 30, 29, 28, 27, 26, 25, 24]
 ORDER2 = [21, 20, 29, 28, 23, 22, 19, 18, 13, 12, 31, 30, 27, 26, 17, 16, 15, 14, 11, 10, 5, 4, 25, 24, 9, 8, 7, 6, 3, 2, 1, 0]
 DLIM = 20
 OUT = jax.ShapeDtypeStruct

time: 35.6 us -> 35.2 us (0.989)
  no operation moved by 1% of the time
where the time goes in v5:
time: 35.2 us; the launch traced here: 35.1 us
  blocking collectives  24.6 us (70%)
  Pallas kernels  10.5 us (30%)
    all_to_all x1, blocking collectives, body(): got = lax.all_to_all(sent, 'seq', 0, 0, axis_index_groups=[list(ORDER1)])  14.1 us
    all_to_all x1, blocking collectives, body(): lax.all_to_all(slot_out, 'seq', 0, 0, axis_index_groups=[list(ORDER2)])  10.4 us
    pallas_call x1, Pallas kernels, dispatch(): pl.pallas_call(functools.partial(dispatch_kernel, chunks), out_shape=(OUT...  4.93 us
    pallas_call x1, Pallas kernels, mix(): pl.pallas_call(functools.partial(mix_kernel, chunks), out_shape=jax.Shape...  3.43 us
    pallas_call x1, Pallas kernels, expert(): pl.pallas_call(expert_kernel, out_shape=jax.ShapeDtypeStruct((devices, sl...  2.15 us

profile of v5, /device:TPU:1, one launch (start us, length us, event | category | flops | bytes accessed | tf_op | source)
XLA Modules:
  0.0 35.1 jit_solution(932731952908973916)
XLA Ops:
  0.0 0.0 copy-start
  0.0 0.0 copy-start.1
  0.0 4.9 %dispatch.1 = (bf16[32,2,1408]{2,1,0:T(2,128)(2,1)S(1)}, f32[2560,64]{1,0:T(8,128)S(1)}) custom-call(bf16[2560,1280]{1,0:T(8,128)(2,1)} %tokens_ref.1, bf16[64,1280]{1,0:T(8,128)(2,1)} %bitcast.1), custom_call_target="tpu_custom_call" | custom-call | flops 6710886400 | bytes 6553600 | tf_op jit(solution)/shard_map/dispatch/pallas_call | solution.py:92
  4.9 14.1 %all_to_all.10.got_ref = bf16[32,2,1408]{2,1,0:T(2,128)(2,1)S(1)} all-to-all(bf16[32,2,1408]{2,1,0:T(2,128)(2,1)S(1)} %get-tuple-element.8), channel_id=1, replica_groups={{23,22,21,20,19,18,17,16,15,14,13,12,11,10,9,8,7,6,5,4,3,2,1,0,31,30,29..., dimensions={0} | all-to-all | bytes 360448 | tf_op jit(solution)/shard_map/all_to_all | solution.py:197
  19.1 0.0 copy-done
  19.1 0.0 copy-done.1
  19.1 2.1 %expert.1 = bf16[32,2,1280]{2,1,0:T(2,128)(2,1)S(1)} custom-call(bf16[32,2,1408]{2,1,0:T(2,128)(2,1)S(1)} %all_to_all.10.got_ref, bf16[1,1280,2560]{2,1,0:T(8,128)(2,1)S(1)} %copy-done, bf16[1,2560,1280]{2,1,0:T(8,128)(2,1)S(1)} %copy-done.1), custom_call_target="tpu_custom_call" | custom-call | flops 26214400 | bytes 13107200 | tf_op jit(solution)/shard_map/expert/pallas_call | solution.py:137
  21.2 10.4 %all_to_all.11.slot_ref = bf16[32,2,1280]{2,1,0:T(2,128)(2,1)S(1)} all-to-all(bf16[32,2,1280]{2,1,0:T(2,128)(2,1)S(1)} %expert.1), channel_id=1, replica_groups={{21,20,29,28,23,22,19,18,13,12,31,30,27,26,17,16,15,14,11,10,5,4,25,24,..., dimensions={0} | all-to-all | bytes 327680 | tf_op jit(solution)/shard_map/all_to_all | solution.py:199
  31.7 3.4 %mix.1 = bf16[2560,1280]{1,0:T(8,128)(2,1)} custom-call(f32[2560,64]{1,0:T(8,128)S(1)} %get-tuple-element.7.logits_ref, bf16[32,2,1280]{2,1,0:T(2,128)(2,1)S(1)} %all_to_all.11.slot_ref), custom_call_target="tpu_custom_call" | custom-call | flops 419430400 | bytes 6553600 | tf_op jit(solution)/shard_map/mix/pallas_call | solution.py:173
Async XLA Ops:
  0.0 19.1 %copy-start = (bf16[1,1280,2560]{2,1,0:T(8,128)(2,1)S(1)}, bf16[1,1280,2560]{2,1,0:T(8,128)(2,1)}, u32[]{:S(2)}) copy-start(bf16[1,1280,2560]{2,1,0:T(8,128)(2,1)} %w_in_ref.1) | copy-start | bytes 19660804
  0.0 19.1 %copy-start.1 = (bf16[1,2560,1280]{2,1,0:T(8,128)(2,1)S(1)}, bf16[1,2560,1280]{2,1,0:T(8,128)(2,1)}, u32[]{:S(2)}) copy-start(bf16[1,2560,1280]{2,1,0:T(8,128)(2,1)} %w_out_ref.1) | copy-start | bytes 19660804

commit v6 on v5

--- a/solution.py
+++ b/solution.py
@@ -10,10 +10,16 @@
 SLOTS = 2
 LANES = 128
 MIB = 1 << 20
-ORDER1 = [23, 22, 21, 20, 19, 18, 17, 16, 15, 14, 13, 12, 11, 10, 9, 8, 7, 6, 5, 4, 3, 2, 1, 0, 31, 30, 29, 28, 27, 26, 25, 24]
-ORDER2 = [21, 20, 29, 28, 23, 22, 19, 18, 13, 12, 31, 30, 27, 26, 17, 16, 15, 14, 11, 10, 5, 4, 25, 24, 9, 8, 7, 6, 3, 2, 1, 0]
-DLIM = 20
-OUT = jax.ShapeDtypeStruct
+SIDE = 4
+
+
+def steps_from_origin(index):
+    x, z = index // (2 * SIDE), index // 2 % SIDE
+    return min(x, SIDE - x) + min(z, SIDE - z)
+
+
+ORDER1 = [(23 - i) % 32 for i in range(32)]
+ORDER2 = sorted(range(32), key=lambda i: (steps_from_origin(i), i), reverse=True)
 
 
 def split3(x):
@@ -92,8 +98,8 @@
     return pl.pallas_call(
         functools.partial(dispatch_kernel, chunks),
         out_shape=(
-            OUT((devices, slots // devices, width + LANES), jnp.bfloat16),
-            OUT((count, slots), jnp.float32),
+            jax.ShapeDtypeStruct((devices, slots // devices, width + LANES), jnp.bfloat16),
+            jax.ShapeDtypeStruct((count, slots), jnp.float32),
         ),
         in_specs=[pl.BlockSpec(memory_space=pltpu.HBM)] * 2,
         out_specs=(pl.BlockSpec(memory_space=pltpu.VMEM), pl.BlockSpec(memory_space=pltpu.VMEM)),
@@ -103,8 +109,10 @@
             pltpu.VMEM((slots, width), jnp.bfloat16),
             pltpu.SemaphoreType.DMA((len(chunks) + 1,)),
         ],
-        compiler_params=pltpu.CompilerParams(vmem_limit_bytes=DLIM * MIB),
-        cost_estimate=pl.CostEstimate(flops=32 * count * width * slots, bytes_accessed=2 * count * width, transcendentals=count * slots),
+        compiler_params=pltpu.CompilerParams(vmem_limit_bytes=20 * MIB),
+        cost_estimate=pl.CostEstimate(
+            flops=32 * count * width * slots, bytes_accessed=2 * count * width, transcendentals=count * slots
+        ),
         name="dispatch",
     )(pltpu.with_memory_space_constraint(tokens, pltpu.HBM), pltpu.with_memory_space_constraint(slot_proj.T, pltpu.HBM))
 
@@ -119,12 +127,14 @@
 def expert_kernel(got_ref, w_in_ref, w_out_ref, out_ref):
     width = w_in_ref.shape[1]
     devices = got_ref.shape[0]
-    got = got_ref[...].astype(jnp.float32)
-    stats = got[:, :, width:]
+    stats = got_ref[:, :, width:].astype(jnp.float32)
     maxes = stats[:, :, 0:1] + stats[:, :, 1:2] + stats[:, :, 2:3]
     totals = stats[:, :, 3:4] + stats[:, :, 4:5] + stats[:, :, 5:6]
     scale = jnp.exp(maxes - jnp.max(maxes, axis=0, keepdims=True))
-    num = jnp.sum(got[:, :, :width] * scale, axis=0)
+    terms = [got_ref[k, :, :width].astype(jnp.float32) * scale[k] for k in range(devices)]
+    while len(terms) > 4:
+        terms = [sum(terms[k + 4 :: 4], terms[k]) for k in range(4)]
+    num = (terms[0] + terms[1]) + (terms[2] + terms[3])
     slot_in = (num / jnp.sum(totals * scale, axis=0)).astype(jnp.bfloat16)
     hidden = jnp.concatenate([jax.nn.gelu(h).astype(jnp.bfloat16) for h in halves_dot(slot_in, w_in_ref)], axis=1)
     out = jnp.concatenate([o.astype(jnp.bfloat16) for o in halves_dot(hidden, w_out_ref)], axis=1)
@@ -139,10 +149,10 @@
         out_shape=jax.ShapeDtypeStruct((devices, slots, w_in.shape[1]), jnp.bfloat16),
         in_specs=[pl.BlockSpec(memory_space=pltpu.VMEM)] * 3,
         out_specs=pl.BlockSpec(memory_space=pltpu.VMEM),
-        compiler_params=pltpu.CompilerParams(vmem_limit_bytes=WLIM * MIB),
+        compiler_params=pltpu.CompilerParams(vmem_limit_bytes=16 * MIB),
         cost_estimate=pl.CostEstimate(flops=4 * slots * w_in.size, bytes_accessed=4 * w_in.size, transcendentals=slots * w_in.shape[2]),
         name="expert",
-    )(got, WC(w_in), WC(w_out))
+    )(got, *(pltpu.with_memory_space_constraint(w, pltpu.VMEM) for w in (w_in, w_out)))
 
 
 def mix_kernel(chunks, logits_ref, slot_ref, mixed_ref, slot_all, held, sem):
@@ -169,7 +179,7 @@
 def mix(logits, slot_all):
     count, slots = logits.shape
     width = slot_all.shape[2]
-    chunks = (count // 10,) * 10
+    chunks = (count // 8,) * 8
     return pl.pallas_call(
         functools.partial(mix_kernel, chunks),
         out_shape=jax.ShapeDtypeStruct((count, width), jnp.bfloat16),
@@ -186,11 +196,6 @@
     )(logits, slot_all)
 
 
-WLIM = 16
-def WC(x):
-    return pltpu.with_memory_space_constraint(x, pltpu.VMEM)
-
-
 def body(tokens, slot_proj, w_in, w_out):
     devices = lax.axis_size("seq")
     sent, logits = dispatch(tokens, slot_proj, devices)

time: 35.2 us -> 35.2 us (level)
  no operation moved by 1% of the time
where the time goes in v6:
time: 35.2 us; the launch traced here: 35 us
  blocking collectives  24.6 us (70%)
  Pallas kernels  10.4 us (30%)
    all_to_all x1, blocking collectives, body(): got = lax.all_to_all(sent, 'seq', 0, 0, axis_index_groups=[list(ORDER1)])  14.1 us
    all_to_all x1, blocking collectives, body(): lax.all_to_all(slot_out, 'seq', 0, 0, axis_index_groups=[list(ORDER2)])  10.4 us
    pallas_call x1, Pallas kernels, dispatch(): pl.pallas_call(functools.partial(dispatch_kernel, chunks), out_shape=(jax...  4.93 us
    pallas_call x1, Pallas kernels, mix(): pl.pallas_call(functools.partial(mix_kernel, chunks), out_shape=jax.Shape...  3.38 us
    pallas_call x1, Pallas kernels, expert(): pl.pallas_call(expert_kernel, out_shape=jax.ShapeDtypeStruct((devices, sl...  2.09 us

profile of v6, /device:TPU:1, one launch (start us, length us, event | category | flops | bytes accessed | tf_op | source)
XLA Modules:
  0.0 35.0 jit_solution(18011287139471132102)
XLA Ops:
  0.0 0.0 copy-start
  0.0 0.0 copy-start.1
  0.0 4.9 %dispatch.1 = (bf16[32,2,1408]{2,1,0:T(2,128)(2,1)S(1)}, f32[2560,64]{1,0:T(8,128)S(1)}) custom-call(bf16[2560,1280]{1,0:T(8,128)(2,1)} %tokens_ref.1, bf16[64,1280]{1,0:T(8,128)(2,1)} %bitcast.1), custom_call_target="tpu_custom_call" | custom-call | flops 6710886400 | bytes 6553600 | tf_op jit(solution)/shard_map/dispatch/pallas_call | solution.py:98
  4.9 14.1 %all_to_all.10.got_ref = bf16[32,2,1408]{2,1,0:T(2,128)(2,1)S(1)} all-to-all(bf16[32,2,1408]{2,1,0:T(2,128)(2,1)S(1)} %get-tuple-element.8), channel_id=1, replica_groups={{23,22,21,20,19,18,17,16,15,14,13,12,11,10,9,8,7,6,5,4,3,2,1,0,31,30,29..., dimensions={0} | all-to-all | bytes 360448 | tf_op jit(solution)/shard_map/all_to_all | solution.py:202
  19.1 0.0 copy-done
  19.1 0.0 copy-done.1
  19.1 2.1 %expert.1 = bf16[32,2,1280]{2,1,0:T(2,128)(2,1)S(1)} custom-call(bf16[32,2,1408]{2,1,0:T(2,128)(2,1)S(1)} %all_to_all.10.got_ref, bf16[1,1280,2560]{2,1,0:T(8,128)(2,1)S(1)} %copy-done, bf16[1,2560,1280]{2,1,0:T(8,128)(2,1)S(1)} %copy-done.1), custom_call_target="tpu_custom_call" | custom-call | flops 26214400 | bytes 13107200 | tf_op jit(solution)/shard_map/expert/pallas_call | solution.py:147
  21.2 10.4 %all_to_all.11.slot_ref = bf16[32,2,1280]{2,1,0:T(2,128)(2,1)S(1)} all-to-all(bf16[32,2,1280]{2,1,0:T(2,128)(2,1)S(1)} %expert.1), channel_id=1, replica_groups={{21,20,29,28,23,22,19,18,13,12,31,30,27,26,17,16,15,14,11,10,5,4,25,24,..., dimensions={0} | all-to-all | bytes 327680 | tf_op jit(solution)/shard_map/all_to_all | solution.py:204
  31.6 3.4 %mix.1 = bf16[2560,1280]{1,0:T(8,128)(2,1)} custom-call(f32[2560,64]{1,0:T(8,128)S(1)} %get-tuple-element.7.logits_ref, bf16[32,2,1280]{2,1,0:T(2,128)(2,1)S(1)} %all_to_all.11.slot_ref), custom_call_target="tpu_custom_call" | custom-call | flops 419430400 | bytes 6553600 | tf_op jit(solution)/shard_map/mix/pallas_call | solution.py:183
Async XLA Ops:
  0.0 19.1 %copy-start = (bf16[1,1280,2560]{2,1,0:T(8,128)(2,1)S(1)}, bf16[1,1280,2560]{2,1,0:T(8,128)(2,1)}, u32[]{:S(2)}) copy-start(bf16[1,1280,2560]{2,1,0:T(8,128)(2,1)} %w_in_ref.1) | copy-start | bytes 19660804
  0.0 19.1 %copy-start.1 = (bf16[1,2560,1280]{2,1,0:T(8,128)(2,1)S(1)}, bf16[1,2560,1280]{2,1,0:T(8,128)(2,1)}, u32[]{:S(2)}) copy-start(bf16[1,2560,1280]{2,1,0:T(8,128)(2,1)} %w_out_ref.1) | copy-start | bytes 19660804

commit v7 on v6

--- a/solution.py
+++ b/solution.py
@@ -37,8 +37,9 @@
         return pltpu.make_async_copy(tokens_ref.at[part], held.at[part], sem.at[i])
 
     proj_copy = pltpu.make_async_copy(proj_hbm, proj_ref, sem.at[len(chunks)])
+    copy(0).start()
     proj_copy.start()
-    for i in range(len(chunks)):
+    for i in range(1, len(chunks)):
         copy(i).start()
     proj_copy.wait()
 
@@ -94,7 +95,7 @@
     count, width = tokens.shape
     slots = slot_proj.shape[1]
     unit = count // 20
-    chunks = (4 * unit, 4 * unit, 6 * unit, 6 * unit)
+    chunks = (3 * unit, 4 * unit, 6 * unit, 7 * unit)
     return pl.pallas_call(
         functools.partial(dispatch_kernel, chunks),
         out_shape=(

time: 35.2 us -> 35.1 us (level)
  no operation moved by 1% of the time
where the time goes in v7:
time: 35.1 us; the launch traced here: 34.9 us
  blocking collectives  24.6 us (70%)
  Pallas kernels  10.3 us (29%)
    all_to_all x1, blocking collectives, body(): got = lax.all_to_all(sent, 'seq', 0, 0, axis_index_groups=[list(ORDER1)])  14.1 us
    all_to_all x1, blocking collectives, body(): lax.all_to_all(slot_out, 'seq', 0, 0, axis_index_groups=[list(ORDER2)])  10.4 us
    pallas_call x1, Pallas kernels, dispatch(): pl.pallas_call(functools.partial(dispatch_kernel, chunks), out_shape=(jax...  4.85 us
    pallas_call x1, Pallas kernels, mix(): pl.pallas_call(functools.partial(mix_kernel, chunks), out_shape=jax.Shape...  3.38 us
    pallas_call x1, Pallas kernels, expert(): pl.pallas_call(expert_kernel, out_shape=jax.ShapeDtypeStruct((devices, sl...  2.09 us

profile of v7, /device:TPU:1, one launch (start us, length us, event | category | flops | bytes accessed | tf_op | source)
XLA Modules:
  0.0 34.9 jit_solution(308462132569423527)
XLA Ops:
  0.0 0.0 copy-start
  0.0 0.0 copy-start.1
  0.0 4.8 %dispatch.1 = (bf16[32,2,1408]{2,1,0:T(2,128)(2,1)S(1)}, f32[2560,64]{1,0:T(8,128)S(1)}) custom-call(bf16[2560,1280]{1,0:T(8,128)(2,1)} %tokens_ref.1, bf16[64,1280]{1,0:T(8,128)(2,1)} %bitcast.1), custom_call_target="tpu_custom_call" | custom-call | flops 6710886400 | bytes 6553600 | tf_op jit(solution)/shard_map/dispatch/pallas_call | solution.py:99
  4.9 14.1 %all_to_all.10.got_ref = bf16[32,2,1408]{2,1,0:T(2,128)(2,1)S(1)} all-to-all(bf16[32,2,1408]{2,1,0:T(2,128)(2,1)S(1)} %get-tuple-element.8), channel_id=1, replica_groups={{23,22,21,20,19,18,17,16,15,14,13,12,11,10,9,8,7,6,5,4,3,2,1,0,31,30,29..., dimensions={0} | all-to-all | bytes 360448 | tf_op jit(solution)/shard_map/all_to_all | solution.py:203
  19.0 0.0 copy-done
  19.0 0.0 copy-done.1
  19.0 2.1 %expert.1 = bf16[32,2,1280]{2,1,0:T(2,128)(2,1)S(1)} custom-call(bf16[32,2,1408]{2,1,0:T(2,128)(2,1)S(1)} %all_to_all.10.got_ref, bf16[1,1280,2560]{2,1,0:T(8,128)(2,1)S(1)} %copy-done, bf16[1,2560,1280]{2,1,0:T(8,128)(2,1)S(1)} %copy-done.1), custom_call_target="tpu_custom_call" | custom-call | flops 26214400 | bytes 13107200 | tf_op jit(solution)/shard_map/expert/pallas_call | solution.py:148
  21.1 10.4 %all_to_all.11.slot_ref = bf16[32,2,1280]{2,1,0:T(2,128)(2,1)S(1)} all-to-all(bf16[32,2,1280]{2,1,0:T(2,128)(2,1)S(1)} %expert.1), channel_id=1, replica_groups={{21,20,29,28,23,22,19,18,13,12,31,30,27,26,17,16,15,14,11,10,5,4,25,24,..., dimensions={0} | all-to-all | bytes 327680 | tf_op jit(solution)/shard_map/all_to_all | solution.py:205
  31.5 3.4 %mix.1 = bf16[2560,1280]{1,0:T(8,128)(2,1)} custom-call(f32[2560,64]{1,0:T(8,128)S(1)} %get-tuple-element.7.logits_ref, bf16[32,2,1280]{2,1,0:T(2,128)(2,1)S(1)} %all_to_all.11.slot_ref), custom_call_target="tpu_custom_call" | custom-call | flops 419430400 | bytes 6553600 | tf_op jit(solution)/shard_map/mix/pallas_call | solution.py:184
Async XLA Ops:
  0.0 19.0 %copy-start = (bf16[1,1280,2560]{2,1,0:T(8,128)(2,1)S(1)}, bf16[1,1280,2560]{2,1,0:T(8,128)(2,1)}, u32[]{:S(2)}) copy-start(bf16[1,1280,2560]{2,1,0:T(8,128)(2,1)} %w_in_ref.1) | copy-start | bytes 19660804
  0.0 19.0 %copy-start.1 = (bf16[1,2560,1280]{2,1,0:T(8,128)(2,1)S(1)}, bf16[1,2560,1280]{2,1,0:T(8,128)(2,1)}, u32[]{:S(2)}) copy-start(bf16[1,2560,1280]{2,1,0:T(8,128)(2,1)} %w_out_ref.1) | copy-start | bytes 19660804

commit v8 on v7

--- a/solution.py
+++ b/solution.py
@@ -68,18 +68,20 @@
             new_top = jnp.maximum(new_top, jnp.max(block, axis=0, keepdims=True))
         fade = jnp.exp(top - new_top)
         total = total * fade
-        adds = []
-        for part, block in zip(halves(i), blocks):
+        weights = []
+        for block in blocks:
             shifted = jnp.exp(block - new_top)
             total = total + jnp.sum(shifted, axis=0, keepdims=True)
-            adds.append(
-                lax.dot_general(
-                    shifted.astype(jnp.bfloat16), held[part, :], (((0,), (0,)), ((), ())),
-                    preferred_element_type=jnp.float32,
-                )
+            weights.append(shifted.astype(jnp.bfloat16))
+        weights = jnp.concatenate(weights, axis=0)
+        kept = fade.reshape(slots, 1)
+        cut = width * 3 // 5
+        for columns in (slice(0, cut), slice(cut, width)):
+            add = lax.dot_general(
+                weights, held[pl.ds(starts[i], chunks[i]), columns], (((0,), (0,)), ((), ())),
+                preferred_element_type=jnp.float32,
             )
-        add = adds[0] + adds[1]
-        acc[...] = add if i == 0 else acc[...] * fade.reshape(slots, 1) + add
+            acc[:, columns] = add if i == 0 else acc[:, columns] * kept + add
         top, blocks = new_top, following
     lanes = [*split3(top), *split3(total)]
     stats = jnp.concatenate([*lanes, jnp.zeros((LANES - len(lanes), slots), jnp.float32)], axis=0)

time: 35.1 us -> 35 us (level)
  no operation moved by 1% of the time
where the time goes in v8:
time: 35 us; the launch traced here: 34.9 us
  blocking collectives  24.6 us (70%)
  Pallas kernels  10.3 us (29%)
    all_to_all x1, blocking collectives, body(): got = lax.all_to_all(sent, 'seq', 0, 0, axis_index_groups=[list(ORDER1)])  14.1 us
    all_to_all x1, blocking collectives, body(): lax.all_to_all(slot_out, 'seq', 0, 0, axis_index_groups=[list(ORDER2)])  10.5 us
    pallas_call x1, Pallas kernels, dispatch(): pl.pallas_call(functools.partial(dispatch_kernel, chunks), out_shape=(jax...  4.81 us
    pallas_call x1, Pallas kernels, mix(): pl.pallas_call(functools.partial(mix_kernel, chunks), out_shape=jax.Shape...  3.38 us
    pallas_call x1, Pallas kernels, expert(): pl.pallas_call(expert_kernel, out_shape=jax.ShapeDtypeStruct((devices, sl...  2.09 us

profile of v8, /device:TPU:1, one launch (start us, length us, event | category | flops | bytes accessed | tf_op | source)
XLA Modules:
  0.0 34.9 jit_solution(16393493688211880982)
XLA Ops:
  0.0 0.0 copy-start
  0.0 0.0 copy-start.1
  0.0 4.8 %dispatch.1 = (bf16[32,2,1408]{2,1,0:T(2,128)(2,1)S(1)}, f32[2560,64]{1,0:T(8,128)S(1)}) custom-call(bf16[2560,1280]{1,0:T(8,128)(2,1)} %tokens_ref.1, bf16[64,1280]{1,0:T(8,128)(2,1)} %bitcast.1), custom_call_target="tpu_custom_call" | custom-call | flops 6710886400 | bytes 6553600 | tf_op jit(solution)/shard_map/dispatch/pallas_call | solution.py:101
  4.8 14.1 %all_to_all.10.got_ref = bf16[32,2,1408]{2,1,0:T(2,128)(2,1)S(1)} all-to-all(bf16[32,2,1408]{2,1,0:T(2,128)(2,1)S(1)} %get-tuple-element.8), channel_id=1, replica_groups={{23,22,21,20,19,18,17,16,15,14,13,12,11,10,9,8,7,6,5,4,3,2,1,0,31,30,29..., dimensions={0} | all-to-all | bytes 360448 | tf_op jit(solution)/shard_map/all_to_all | solution.py:205
  18.9 0.0 copy-done
  18.9 0.0 copy-done.1
  18.9 2.1 %expert.1 = bf16[32,2,1280]{2,1,0:T(2,128)(2,1)S(1)} custom-call(bf16[32,2,1408]{2,1,0:T(2,128)(2,1)S(1)} %all_to_all.10.got_ref, bf16[1,1280,2560]{2,1,0:T(8,128)(2,1)S(1)} %copy-done, bf16[1,2560,1280]{2,1,0:T(8,128)(2,1)S(1)} %copy-done.1), custom_call_target="tpu_custom_call" | custom-call | flops 26214400 | bytes 13107200 | tf_op jit(solution)/shard_map/expert/pallas_call | solution.py:150
  21.0 10.5 %all_to_all.11.slot_ref = bf16[32,2,1280]{2,1,0:T(2,128)(2,1)S(1)} all-to-all(bf16[32,2,1280]{2,1,0:T(2,128)(2,1)S(1)} %expert.1), channel_id=1, replica_groups={{21,20,29,28,23,22,19,18,13,12,31,30,27,26,17,16,15,14,11,10,5,4,25,24,..., dimensions={0} | all-to-all | bytes 327680 | tf_op jit(solution)/shard_map/all_to_all | solution.py:207
  31.5 3.4 %mix.1 = bf16[2560,1280]{1,0:T(8,128)(2,1)} custom-call(f32[2560,64]{1,0:T(8,128)S(1)} %get-tuple-element.7.logits_ref, bf16[32,2,1280]{2,1,0:T(2,128)(2,1)S(1)} %all_to_all.11.slot_ref), custom_call_target="tpu_custom_call" | custom-call | flops 419430400 | bytes 6553600 | tf_op jit(solution)/shard_map/mix/pallas_call | solution.py:186
Async XLA Ops:
  0.0 18.9 %copy-start = (bf16[1,1280,2560]{2,1,0:T(8,128)(2,1)S(1)}, bf16[1,1280,2560]{2,1,0:T(8,128)(2,1)}, u32[]{:S(2)}) copy-start(bf16[1,1280,2560]{2,1,0:T(8,128)(2,1)} %w_in_ref.1) | copy-start | bytes 19660804
  0.0 18.9 %copy-start.1 = (bf16[1,2560,1280]{2,1,0:T(8,128)(2,1)S(1)}, bf16[1,2560,1280]{2,1,0:T(8,128)(2,1)}, u32[]{:S(2)}) copy-start(bf16[1,2560,1280]{2,1,0:T(8,128)(2,1)} %w_out_ref.1) | copy-start | bytes 19660804

commit v9 on v7

--- a/solution.py
+++ b/solution.py
@@ -170,7 +170,7 @@
         for part in [pl.ds(starts[i] + k * rows, rows) for k in range(2)]:
             block = logits_ref[part, :]
             shifted = jnp.exp(block - jnp.max(block, axis=1, keepdims=True))
-            combine = (shifted / jnp.sum(shifted, axis=1, keepdims=True)).astype(jnp.bfloat16)
+            combine = (shifted * (1.0 / jnp.sum(shifted, axis=1, keepdims=True))).astype(jnp.bfloat16)
             held[part, :] = jnp.dot(combine, slot_all[...], preferred_element_type=jnp.float32).astype(jnp.bfloat16)
         copy(i).start()
     for i in range(len(chunks)):

time: 35.1 us -> 35.1 us (level)
  no operation moved by 1% of the time
where the time goes in v9:
time: 35.1 us; the launch traced here: 34.9 us
  blocking collectives  24.6 us (70%)
  Pallas kernels  10.3 us (29%)
    all_to_all x1, blocking collectives, body(): got = lax.all_to_all(sent, 'seq', 0, 0, axis_index_groups=[list(ORDER1)])  14.1 us
    all_to_all x1, blocking collectives, body(): lax.all_to_all(slot_out, 'seq', 0, 0, axis_index_groups=[list(ORDER2)])  10.4 us
    pallas_call x1, Pallas kernels, dispatch(): pl.pallas_call(functools.partial(dispatch_kernel, chunks), out_shape=(jax...  4.85 us
    pallas_call x1, Pallas kernels, mix(): pl.pallas_call(functools.partial(mix_kernel, chunks), out_shape=jax.Shape...  3.38 us
    pallas_call x1, Pallas kernels, expert(): pl.pallas_call(expert_kernel, out_shape=jax.ShapeDtypeStruct((devices, sl...  2.09 us

profile of v9, /device:TPU:1, one launch (start us, length us, event | category | flops | bytes accessed | tf_op | source)
XLA Modules:
  0.0 34.9 jit_solution(308462132569423527)
XLA Ops:
  0.0 0.0 copy-start
  0.0 0.0 copy-start.1
  0.0 4.8 %dispatch.1 = (bf16[32,2,1408]{2,1,0:T(2,128)(2,1)S(1)}, f32[2560,64]{1,0:T(8,128)S(1)}) custom-call(bf16[2560,1280]{1,0:T(8,128)(2,1)} %tokens_ref.1, bf16[64,1280]{1,0:T(8,128)(2,1)} %bitcast.1), custom_call_target="tpu_custom_call" | custom-call | flops 6710886400 | bytes 6553600 | tf_op jit(solution)/shard_map/dispatch/pallas_call | solution.py:99
  4.9 14.1 %all_to_all.10.got_ref = bf16[32,2,1408]{2,1,0:T(2,128)(2,1)S(1)} all-to-all(bf16[32,2,1408]{2,1,0:T(2,128)(2,1)S(1)} %get-tuple-element.8), channel_id=1, replica_groups={{23,22,21,20,19,18,17,16,15,14,13,12,11,10,9,8,7,6,5,4,3,2,1,0,31,30,29..., dimensions={0} | all-to-all | bytes 360448 | tf_op jit(solution)/shard_map/all_to_all | solution.py:203
  19.0 0.0 copy-done
  19.0 0.0 copy-done.1
  19.0 2.1 %expert.1 = bf16[32,2,1280]{2,1,0:T(2,128)(2,1)S(1)} custom-call(bf16[32,2,1408]{2,1,0:T(2,128)(2,1)S(1)} %all_to_all.10.got_ref, bf16[1,1280,2560]{2,1,0:T(8,128)(2,1)S(1)} %copy-done, bf16[1,2560,1280]{2,1,0:T(8,128)(2,1)S(1)} %copy-done.1), custom_call_target="tpu_custom_call" | custom-call | flops 26214400 | bytes 13107200 | tf_op jit(solution)/shard_map/expert/pallas_call | solution.py:148
  21.1 10.4 %all_to_all.11.slot_ref = bf16[32,2,1280]{2,1,0:T(2,128)(2,1)S(1)} all-to-all(bf16[32,2,1280]{2,1,0:T(2,128)(2,1)S(1)} %expert.1), channel_id=1, replica_groups={{21,20,29,28,23,22,19,18,13,12,31,30,27,26,17,16,15,14,11,10,5,4,25,24,..., dimensions={0} | all-to-all | bytes 327680 | tf_op jit(solution)/shard_map/all_to_all | solution.py:205
  31.5 3.4 %mix.1 = bf16[2560,1280]{1,0:T(8,128)(2,1)} custom-call(f32[2560,64]{1,0:T(8,128)S(1)} %get-tuple-element.7.logits_ref, bf16[32,2,1280]{2,1,0:T(2,128)(2,1)S(1)} %all_to_all.11.slot_ref), custom_call_target="tpu_custom_call" | custom-call | flops 419430400 | bytes 6553600 | tf_op jit(solution)/shard_map/mix/pallas_call | solution.py:184
Async XLA Ops:
  0.0 19.0 %copy-start = (bf16[1,1280,2560]{2,1,0:T(8,128)(2,1)S(1)}, bf16[1,1280,2560]{2,1,0:T(8,128)(2,1)}, u32[]{:S(2)}) copy-start(bf16[1,1280,2560]{2,1,0:T(8,128)(2,1)} %w_in_ref.1) | copy-start | bytes 19660804
  0.0 19.0 %copy-start.1 = (bf16[1,2560,1280]{2,1,0:T(8,128)(2,1)S(1)}, bf16[1,2560,1280]{2,1,0:T(8,128)(2,1)}, u32[]{:S(2)}) copy-start(bf16[1,2560,1280]{2,1,0:T(8,128)(2,1)} %w_out_ref.1) | copy-start | bytes 19660804
